TPU v7x, 512 devices: a whole 4x8x8 slice. The times are simulated.
512 devices in a mesh: dp: 128 (over y, z, core), tensor: 4 (over x).
Axes of the slice: x: 4, y: 8, z: 8, core: 2. Of those that a mesh axis runs over, the one named last changes fastest.
Arguments:
- tokens_in: bfloat16 [75776, 256], P(('dp', 'tensor')), as said below
- grad_hidden: bfloat16 [75776, 16384], P('dp', 'tensor'), as said below
Outputs:
- decoded: float32 [256, 16384], P('dp', 'tensor')
- code_total: float32 [256, 16384], P('dp', 'tensor')
Inputs may be any that keep to these rules, and one draw needn't show every extreme that they name: `tokens_in`: features of a token, of order one. `grad_hidden`: gradients of order one over the square root of 75776.
All inputs are finite; a program needn't handle non-finite values.
Results may differ from a plain program's by a relative error of at most 0.0065.
Values may be sent and summed in bfloat16 or wider, within the bound.
A program may use at most 64 MiB of HBM per device.

v0:
```python
import jax
import jax.numpy as jnp
import numpy as np
from jax import lax
from jax.sharding import PartitionSpec as P

HAD = 128


epsilon = 1e-06
code_limit = 448.0
clip_ratio = 2.0


def hadamard_table(points):
    index = np.arange(points)
    both = index[:, None] & index[None, :]
    parity = np.zeros((points, points), np.int64)
    for shift in range(16):
        parity = parity + (both >> shift & 1)
    return (np.where(parity % 2 == 0, 1.0, -1.0) / np.sqrt(points)).astype(np.float32)


def rotate_rows(partial_value):
    table = jnp.asarray(hadamard_table(HAD), jnp.float32)
    rows, width = partial_value.shape
    blocks = partial_value.reshape(rows, width // HAD, HAD)
    turned = jnp.einsum("rbk,kj->rbj", blocks, table, precision=lax.Precision.HIGHEST)
    return turned.reshape(rows, width)


def rotated_part(inputs, grads):
    partial_value = lax.dot_general(
        inputs, grads, (((0,), (0,)), ((), ())), preferred_element_type=jnp.float32
    )
    return rotate_rows(partial_value)


def local(tokens_in, grad_hidden):
    inputs = lax.all_gather(tokens_in, "tensor", axis=0, tiled=True)
    half_width = grad_hidden.shape[1] // 2
    rotated = rotated_part(inputs, grad_hidden)
    grouped = rotated.reshape(rotated.shape[0], 2, half_width)
    local_peak = jnp.sqrt(jnp.mean(jnp.square(grouped), axis=2) + epsilon)
    row_peak = lax.pmax(local_peak, "dp")
    row_scale = clip_ratio * row_peak / code_limit
    row_count = rotated.shape[0]
    scaled = rotated.reshape(row_count, 2, half_width) / row_scale[:, :, None]
    coded = (
        jnp.clip(scaled, -code_limit, code_limit)
        .astype(jnp.bfloat16)
        .reshape(row_count, 2 * half_width)
    )
    devices = lax.axis_size("dp")
    own_rows = row_count // devices
    summed = lax.psum_scatter(coded.astype(jnp.float32), "dp", scatter_dimension=0, tiled=True)
    own_scale = lax.dynamic_slice_in_dim(row_scale, lax.axis_index("dp") * own_rows, own_rows, 0)
    decoded = (summed.reshape(own_rows, 2, half_width) * own_scale[:, :, None]).reshape(
        own_rows, 2 * half_width
    )
    return (decoded, summed / code_limit)


def solution(mesh):
    placed = (P(("dp", "tensor"), None), P("dp", "tensor"))
    return jax.shard_map(
        local,
        mesh=mesh,
        in_specs=placed,
        out_specs=(P("dp", "tensor"), P("dp", "tensor")),
        check_vma=False,
    )
```

profile of v0, /device:TPU:1, one launch (start us, length us, event | category | flops | bytes accessed | tf_op | source)
XLA Modules:
  0.0 506.5 jit_solution(12215828446022145337)
XLA Ops:
  7.2 0.0 all-reduce.3.cloned.1.call-start
  7.2 10.9 %all-gather = bf16[4,148,256]{2,1,0:T(8,128)(2,1)S(1)} all-gather(bf16[1,148,256]{2,1,0:T(8,128)(2,1)} %bitcast.25), channel_id=1, replica_groups=mesh['dp'=128,'tensor'=4] {'tensor'}, dimensions={0}, use_global_device_ids=true | all-gather | bytes 378880 | tf_op jit(solution)/shard_map/all_gather | solution.py:40
  18.1 0.1 reshape.18
  18.1 0.0 copy-start.1
  18.1 4.3 convolution_bitcast_fusion
  22.4 0.0 copy-done.1
  22.4 6.0 %multiply_reduce_fusion = (f32[256,32]{0,1:T(8,128)S(1)}, f32[256,32,128]{0,2,1:T(8,128)}) fusion(f32[128,128,1]{0,1,2:T(8,128)S(1)} %copy-done.1, f32[32,32,8,128]{3,2,1,0:T(8,128)S(1)} %convolution_bitcast_fusion), kind=kOutput, calls=%fused_computation.4 | convolution fusion | flops 1612701696 | bytes 8486912 | tf_op jit(solution)/shard_map/rbk,kj->rbj/dot_general | solution.py:28
  28.4 5.6 %copy.11 = f32[256,4096]{1,0:T(8,128)} copy(f32[256,4096]{0,1:T(8,128)} %bitcast.22) | data formatting | bytes 8388608 | tf_op jit(solution)/shard_map/reshape;reshape | solution.py:48
  34.1 256.9 %pmax.7 = f32[256,2]{0,1:T(2,128)S(1)} all-reduce(f32[256,2]{0,1:T(2,128)S(1)} %add_sqrt_fusion), channel_id=1, replica_groups=mesh['dp'=128,'tensor'=4] {'dp'}, use_global_device_ids=true, to_apply=%region_2.3 | all-reduce | flops 512 | bytes 4096 | tf_op jit(solution)/shard_map/pmax | solution.py:45
  291.0 0.1 copy.10
  291.2 1.1 div.33
  292.3 0.0 copy-start
  292.3 3.9 copy.14
  296.2 0.0 copy-done
  296.2 2.6 fusion.3
  298.8 0.0 all-reduce.3.cloned.1.call-update
  298.9 0.1 constant_dynamic-slice_fusion
  298.9 0.1 copy.12
  299.0 0.1 broadcast_bitcast_fusion
  299.2 1.3 dynamic-slice
  301.1 197.1 %all-reduce.3.cloned.1.call-done = f32[256,4096]{1,0:T(8,128)} async-done(((f32[256,4096]{1,0:T(8,128)}), f32[256,4096]{1,0:T(8,128)}) %all-reduce.3.cloned.1.call-update) | async-done | bytes 4194320
  498.1 1.6 dynamic-slice_multiply_fusion
  (4 shorter events, 0.1 us)
Async XLA Ops:
  7.2 491.0 %all-reduce.3.cloned.1.call-start = ((), (), s32[]{:S(2)}) async-start(), calls=%async_computation | async-start | bytes 8388608
  18.1 4.3 copy-start.1
  292.3 3.9 copy-start
Sparse Core Ops, SparseCore 0:
  299.0 199.1 all-reduce.2
where the time goes:
time: 508 us; the launch traced here: 507 us
  blocking collectives  268 us (53%)
  waiting for transfers between devices  197 us (39%)
  between operations  14.8 us (3%)
  local copies, waits for them, and re-layouts  12.4 us (2%)
  matrix products  10.3 us (2%)
    pmax x1, blocking collectives, local(): row_peak = lax.pmax(local_peak, 'dp')  257 us
    unnamed x2, waiting for transfers between devices  197 us
    all_gather x1, blocking collectives, local(): inputs = lax.all_gather(tokens_in, 'tensor', axis=0, tiled=True)  10.9 us
  transfers between devices with their start and end apart: 1, of which 1 were waited for; matrix products, arithmetic and copies ran while one was open for 0% of the time, Pallas kernels for 0%

commit v1 on v0

v1 whole, which is shorter than its diff:
```python
import jax
import jax.numpy as jnp
from jax import lax
from jax.experimental import pallas as pl
from jax.experimental.pallas import tpu as pltpu
from jax.sharding import PartitionSpec as P

NY = 8
NZ = 8
NT = 4
TOKENS = 148
STEP = 144
SLOT = 160
DEPTH = 592
ROWS = 256
HALF = 128
HID = 4096
GROUP = 2048
EPS = 1e-06
F32 = jnp.float32
BF16 = jnp.bfloat16
MESH = pl.DeviceIdType.MESH
FAR_FIRST = (4, 3, 5, 2, 6, 1, 7)


def row_order(group):
    new = lax.broadcasted_iota(jnp.int32, (ROWS, ROWS), 0)
    old = lax.broadcasted_iota(jnp.int32, (ROWS, ROWS), 1)
    core, first, second, i = new >> 7, (new >> 4) & 7, (new >> 1) & 7, new & 1
    y, z = (first, second) if group == 0 else (second, first)
    return jnp.where(old == 32 * y + 4 * z + 2 * core + i, 1.0, 0.0).astype(BF16)


def hadamard_pair():
    row = lax.broadcasted_iota(jnp.int32, (256, 256), 0)
    column = lax.broadcasted_iota(jnp.int32, (256, 256), 1)
    both = row & column & 127
    both = both ^ (both >> 4)
    both = both ^ (both >> 2)
    both = both ^ (both >> 1)
    sign = jnp.where((both & 1) == 0, 0.0625, -0.0625)
    return jnp.where((row >> 7) == (column >> 7), sign, 0.0).astype(BF16)


def kernel(
    tok_ref, grad_ref, dec_ref, tot_ref,
    slots, gbuf, feat, turned, part, rot, other, squares,
    qall, qfirst, q1, q2, peak, inv, code, land1, acc, w, pack, land2,
    gsem, tsend, trecv, q1send, q1recv, q2send, q2recv, xsend, xrecv,
    send1, recv1, send2, recv2,
):
    dp = lax.axis_index("dp")
    t = lax.axis_index("tensor")
    c = lax.rem(dp, 2)
    z = lax.rem(lax.div(dp, 2), NZ)
    y = lax.div(dp, 2 * NZ)
    oc = 1 - c

    def device(yy, zz, cc):
        return (yy * (2 * NZ) + zz * 2 + cc, t)

    def shift(value, k, n):
        return lax.rem(value + k, n)

    grad_copy = pltpu.make_async_copy(grad_ref, gbuf, gsem)
    grad_copy.start()

    barrier = pltpu.get_barrier_semaphore()
    peers_t = [(dp, shift(t, k, NT)) for k in range(1, NT)]
    peers_1 = [
        (kz * 2 + kc, shift(c, kc, 2), device(y, shift(z, kz, NZ), shift(c, kc, 2)))
        for kz in range(NZ)
        for kc in range(2)
        if kz + kc > 0
    ]
    peers_y = [device(shift(y, k, NY), z, c) for k in range(1, NY)]
    everyone = peers_t + [p[2] for p in peers_1] + peers_y
    for peer in everyone:
        pl.semaphore_signal(barrier, inc=1, device_id=peer, device_id_type=MESH)
    slots[t] = tok_ref[...]
    table = hadamard_pair()
    pl.semaphore_wait(barrier, len(everyone))

    token_copies = []
    for k in range(1, NT):
        copy = pltpu.make_async_remote_copy(
            src_ref=slots.at[t], dst_ref=slots.at[t],
            send_sem=tsend.at[k], recv_sem=trecv.at[t],
            device_id=(dp, shift(t, k, NT)), device_id_type=MESH,
        )
        copy.start()
        token_copies.append(copy)
    for k in range(1, NT):
        source = shift(t, k, NT)
        pltpu.make_async_remote_copy(
            src_ref=slots.at[source], dst_ref=slots.at[source],
            send_sem=tsend.at[k], recv_sem=trecv.at[source],
            device_id=(dp, source), device_id_type=MESH,
        ).wait_recv()
    feat[0:STEP, :] = slots[0, 0:STEP, :]
    for s in range(1, NT):
        feat[s * STEP:s * STEP + 16, :] = (
            slots[s - 1, STEP:SLOT, :].astype(F32) + slots[s, 0:16, :].astype(F32)
        ).astype(BF16)
        last = SLOT if s == NT - 1 else STEP
        feat[s * STEP + 16:s * STEP + last, :] = slots[s, 16:last, :]
    features = feat[...]
    for g in range(2):
        turned[g] = lax.dot_general(
            row_order(g), features, (((1,), (1,)), ((), ())), preferred_element_type=F32
        ).astype(BF16)

    grad_copy.wait()
    ones = jnp.ones((8, 128), F32)
    for g in range(2):
        left = turned[g]
        for tile in range(GROUP // 256):
            at = g * GROUP + tile * 256
            value = jnp.dot(left, gbuf[:, at:at + 256], preferred_element_type=F32)
            part[:, at:at + 256] = value
            both = value[:, :128] * value[:, :128] + value[:, 128:] * value[:, 128:]
            squares[...] = both if tile == 0 else squares[...] + both
        q = lax.dot_general(
            ones, squares[...], (((1,), (1,)), ((), ())),
            preferred_element_type=F32, precision=lax.Precision.HIGHEST,
        )
        for half in range(2):
            qall[half, g:g + 1, :] = q[0:1, half * HALF:(half + 1) * HALF]

    for slot, core, peer in peers_1:
        pltpu.make_async_remote_copy(
            src_ref=qall.at[core], dst_ref=q1.at[slot],
            send_sem=q1send, recv_sem=q1recv, device_id=peer, device_id_type=MESH,
        ).start()

    def rotate(half, g, j):
        rows = pl.ds(pl.multiple_of(half * HALF, HALF), HALF)
        at = g * GROUP + j * 1024
        value = jnp.concatenate(
            [part[rows, at + n * 256:at + (n + 1) * 256] for n in range(4)], axis=0
        )
        high = value.astype(BF16)
        low = (value - high.astype(F32)).astype(BF16)
        result = (
            jnp.dot(high, table, preferred_element_type=F32)
            + jnp.dot(low, table, preferred_element_type=F32)
        ).astype(BF16)
        for n in range(4):
            rot[g, rows, j * 1024 + n * 256:j * 1024 + (n + 1) * 256] = (
                result[n * HALF:(n + 1) * HALF]
            )

    def cross(g, j):
        return pltpu.make_async_remote_copy(
            src_ref=rot.at[g, pl.ds(pl.multiple_of(oc * HALF, HALF), HALF), pl.ds(j * 1024, 1024)],
            dst_ref=other.at[g, :, pl.ds(j * 1024, 1024)],
            send_sem=xsend.at[g * 2 + j], recv_sem=xrecv.at[g * 2 + j],
            device_id=device(y, z, oc), device_id_type=MESH,
        )

    for g in range(2):
        for j in range(2):
            rotate(oc, g, j)
            cross(g, j).start()

    q1_all = pltpu.make_async_remote_copy(
        src_ref=q1.at[pl.ds(1, 15)], dst_ref=q1.at[pl.ds(1, 15)],
        send_sem=q1send, recv_sem=q1recv, device_id=device(y, z, oc), device_id_type=MESH,
    )
    q1_all.wait_recv()
    best = qall[c]
    for slot in range(1, 16):
        best = jnp.maximum(best, q1[slot])
    qfirst[...] = best
    for k in range(1, NY):
        pltpu.make_async_remote_copy(
            src_ref=qfirst, dst_ref=q2.at[k],
            send_sem=q2send, recv_sem=q2recv, device_id=peers_y[k - 1], device_id_type=MESH,
        ).start()
    for g in range(2):
        for j in range(2):
            rotate(c, g, j)
    q2_all = pltpu.make_async_remote_copy(
        src_ref=q2.at[pl.ds(1, 7)], dst_ref=q2.at[pl.ds(1, 7)],
        send_sem=q2send, recv_sem=q2recv, device_id=peers_y[0], device_id_type=MESH,
    )
    q2_all.wait_recv()
    best = qfirst[...]
    for k in range(1, NY):
        best = jnp.maximum(best, q2[k])
    best = jnp.sqrt(best / float(GROUP) + EPS)
    for g in range(2):
        wide = jnp.transpose(jnp.broadcast_to(best[g:g + 1, :], (HALF, 128)))
        peak[g] = wide
        inv[g] = 0.7071067811865476 / wide
    for g in range(2):
        for j in range(2):
            cross(g, j).wait_recv()

    def coded(g, k):
        place = shift((y, z)[g], k, 8)
        rows = pl.ds(pl.multiple_of(place * 16, 16), 16)
        mine = pl.ds(pl.multiple_of(c * HALF + place * 16, 16), 16)
        scale = jnp.concatenate([inv[g, rows, :]] * (GROUP // 128), axis=1)
        own = jnp.clip(rot[g, mine, :].astype(F32) * scale, -1.0, 1.0)
        return own + jnp.clip(other[g, rows, :].astype(F32) * scale, -1.0, 1.0)

    def first(g, k):
        peer = device(shift(y, k, NY), z, c) if g == 0 else device(y, shift(z, k, NZ), c)
        return pltpu.make_async_remote_copy(
            src_ref=code.at[g, k], dst_ref=land1.at[g, k],
            send_sem=send1.at[g, k], recv_sem=recv1.at[g, k],
            device_id=peer, device_id_type=MESH,
        )

    for k in FAR_FIRST:
        for g in range(2):
            code[g, k] = coded(g, k).astype(BF16)
            first(g, k).start()
    for g in range(2):
        acc[g] = coded(g, 0)

    def second(g, k):
        peer = device(y, shift(z, k, NZ), c) if g == 0 else device(shift(y, k, NY), z, c)
        return pltpu.make_async_remote_copy(
            src_ref=pack.at[g, shift((z, y)[g], k, 8)], dst_ref=land2.at[g, k],
            send_sem=send2.at[g, k], recv_sem=recv2.at[g, k],
            device_id=peer, device_id_type=MESH,
        )

    for k in FAR_FIRST:
        for g in range(2):
            first(g, k).wait_recv()
            acc[g] = acc[g] + land1[g, k].astype(F32)
    for g in range(2):
        for block in range(16):
            w[g, block * 16:(block + 1) * 16, :] = acc[g, :, block * 128:(block + 1) * 128]
        for place in range(8):
            pack[g, place] = jnp.concatenate(
                [w[g, pl.ds(place * 2 + i, 16, stride=16), :] for i in range(2)], axis=0
            ).astype(BF16)
        for k in FAR_FIRST:
            second(g, k).start()

    for g in range(2):
        total = pack[g, (z, y)[g]].astype(F32)
        for k in FAR_FIRST:
            second(g, k).wait_recv()
            total = total + land2[g, k].astype(F32)
        for i in range(2):
            row = (y, z)[g] * 16 + (z, y)[g] * 2 + i
            value = total[i * 16:(i + 1) * 16]
            at = i * 32 + g * 16
            tot_ref[at:at + 16, :] = value
            dec_ref[at:at + 16, :] = value * (2.0 * peak[g, pl.ds(row, 1), :])

    for copy in token_copies:
        copy.wait_send()
    q1_all.wait_send()
    q2_all.wait_send()
    for g in range(2):
        for j in range(2):
            cross(g, j).wait_send()
        for k in FAR_FIRST:
            first(g, k).wait_send()
            second(g, k).wait_send()


def local(tokens_in, grad_hidden):
    start = 4 * lax.axis_index("tensor")
    slot = lax.dynamic_update_slice(
        jnp.zeros((SLOT, ROWS), BF16), tokens_in, (start, jnp.zeros_like(start))
    )
    dma = pltpu.SemaphoreType.DMA
    decoded, total = pl.pallas_call(
        kernel,
        out_shape=[jax.ShapeDtypeStruct((64, 128), F32)] * 2,
        in_specs=[
            pl.BlockSpec(memory_space=pltpu.VMEM),
            pl.BlockSpec(memory_space=pl.ANY),
        ],
        out_specs=[pl.BlockSpec(memory_space=pltpu.VMEM)] * 2,
        scratch_shapes=[
            pltpu.VMEM((NT, SLOT, ROWS), BF16),
            pltpu.VMEM((DEPTH, HID), BF16),
            pltpu.VMEM((DEPTH, ROWS), BF16),
            pltpu.VMEM((2, ROWS, DEPTH), BF16),
            pltpu.VMEM((ROWS, HID), F32),
            pltpu.VMEM((2, ROWS, GROUP), BF16),
            pltpu.VMEM((2, HALF, GROUP), BF16),
            pltpu.VMEM((ROWS, 128), F32),
            pltpu.VMEM((2, 2, 128), F32),
            pltpu.VMEM((2, 128), F32),
            pltpu.VMEM((16, 2, 128), F32),
            pltpu.VMEM((8, 2, 128), F32),
            pltpu.VMEM((2, HALF, 128), F32),
            pltpu.VMEM((2, HALF, 128), F32),
            pltpu.VMEM((2, 8, 16, GROUP), BF16),
            pltpu.VMEM((2, 8, 16, GROUP), BF16),
            pltpu.VMEM((2, 16, GROUP), F32),
            pltpu.VMEM((2, 256, 128), F32),
            pltpu.VMEM((2, 8, 32, 128), BF16),
            pltpu.VMEM((2, 8, 32, 128), BF16),
            dma, dma((NT,)), dma((NT,)), dma, dma, dma, dma, dma((4,)), dma((4,)),
            dma((2, 8)), dma((2, 8)), dma((2, 8)), dma((2, 8)),
        ],
        compiler_params=pltpu.CompilerParams(
            collective_id=0, has_side_effects=True, vmem_limit_bytes=48 * 1024 * 1024
        ),
        cost_estimate=pl.CostEstimate(
            flops=2 * DEPTH * ROWS * HID, bytes_accessed=2 * DEPTH * HID, transcendentals=0
        ),
    )(slot, grad_hidden)
    return decoded.reshape(2, HID), total.reshape(2, HID)


def solution(mesh):
    placed = (P(("dp", "tensor"), None), P("dp", "tensor"))
    return jax.shard_map(
        local,
        mesh=mesh,
        in_specs=placed,
        out_specs=(P("dp", "tensor"), P("dp", "tensor")),
        check_vma=False,
    )
```

time: 508 us -> 57.5 us (0.11)
  blocking collectives: 268 us -> 0 us
  waiting for transfers between devices: 197 us -> 0 us
  Pallas kernels: 0 us -> 51.7 us
  between operations: 14.8 us -> 0.66 us
  matrix products: 10.3 us -> 0 us
  local copies, waits for them, and re-layouts: 12.4 us -> 4.97 us
    pmax x1 -> x0, blocking collectives: 257 us -> none  [local(): row_peak = lax.pmax(local_peak, 'dp')]
    unnamed x2 -> x0, waiting for transfers between devices: 197 us -> none
    pallas_call x0 -> x1, Pallas kernels: none -> 51.7 us  [local(): pl.pallas_call(kernel, out_shape=[jax.ShapeDtypeStruct((64, 128), F32)] *...]
    all_gather x1 -> x0, blocking collectives: 10.9 us -> none  [local(): inputs = lax.all_gather(tokens_in, 'tensor', axis=0, tiled=True)]
    dot_general x2 -> x0, matrix products: 10.3 us -> none  [the longest x1 5.99 us: rotate_rows(): jnp.einsum('rbk,kj->rbj', blocks, table, precision=lax.Precision.HIGHEST)]
    another operation x1 -> x0, local copies, waits for them, and re-layouts: 5.65 us -> none  [local(): scaled = rotated.reshape(row_count, 2, half_width) / row_scale[:, :, None]]
  transfers between devices with their start and end apart: 1 -> 0, of which waited for: 1 -> 0; matrix products, arithmetic and copies ran while one was open for 0% -> 0% of each run, Pallas kernels for 0% -> 0%
where the time goes in v1:
time: 57.5 us; the launch traced here: 57.3 us
  Pallas kernels  51.7 us (90%)
  local copies, waits for them, and re-layouts  4.97 us (9%)
  between operations  0.66 us (1%)
    pallas_call x1, Pallas kernels, local(): pl.pallas_call(kernel, out_shape=[jax.ShapeDtypeStruct((64, 128), F32)] *...  51.7 us
    unnamed x2, local copies, waits for them, and re-layouts  2.37 us
    dynamic_update_slice x1, local copies, waits for them, and re-layouts, local(): lax.dynamic_update_slice(jnp.zeros((SLOT, ROWS), BF16), tokens_in, (start...  1.32 us
    reshape x2, local copies, waits for them, and re-layouts, local(): return (decoded.reshape(2, HID), total.reshape(2, HID))  1.27 us

profile of v1, /device:TPU:1, one launch (start us, length us, event | category | flops | bytes accessed | tf_op | source)
XLA Modules:
  0.0 57.3 jit_solution(2628470623528849390)
XLA Ops:
  0.6 1.3 %dynamic_update_slice.3.tok_ref = bf16[160,256]{1,0:T(8,128)(2,1)S(1)} dynamic-update-slice(bf16[160,256]{1,0:T(8,128)(2,1)S(1)} %broadcast_in_dim.3, bf16[148,256]{1,0:T(8,128)(2,1)} %param.2, s32[]{:T(128)S(6)} %select_n.3, s32[]{:T(128)} %constant.3.clone.1) | dynamic-update-slice | bytes 151556 | tf_op jit(solution)/shard_map/dynamic_update_slice | solution.py:271
  2.0 0.0 copy-start
  2.0 2.4 %copy-done = bf16[592,4096]{1,0:T(8,128)(2,1)S(1)} copy-done((bf16[592,4096]{1,0:T(8,128)(2,1)S(1)}, bf16[592,4096]{1,0:T(8,128)(2,1)}, u32[]{:S(2)}) %copy-start) | copy-done | bytes 4849688
  4.4 51.7 %shard_map.41 = (f32[64,128]{1,0:T(8,128)S(1)}, f32[64,128]{1,0:T(8,128)S(1)}) custom-call(bf16[160,256]{1,0:T(8,128)(2,1)S(1)} %dynamic_update_slice.3.tok_ref, bf16[592,4096]{1,0:T(8,128)(2,1)S(1)} %copy-done), custom_call_target="tpu_custom_call" | custom-call | flops 1241513984 | bytes 4849664 | tf_op jit(solution)/shard_map/pallas_call | solution.py:275
  56.0 0.6 %reshape.10 = f32[2,4096]{1,0:T(2,128)} reshape(f32[64,128]{1,0:T(8,128)S(1)} %get-tuple-element.4) | data formatting | bytes 65536 | tf_op jit(solution)/shard_map/reshape | solution.py:314
  56.7 0.6 %reshape.11 = f32[2,4096]{1,0:T(2,128)} reshape(f32[64,128]{1,0:T(8,128)S(1)} %get-tuple-element.5) | data formatting | bytes 65536 | tf_op jit(solution)/shard_map/reshape | solution.py:314
  (1 shorter events, 0.0 us)
Async XLA Ops:
  2.0 2.4 %copy-start = (bf16[592,4096]{1,0:T(8,128)(2,1)S(1)}, bf16[592,4096]{1,0:T(8,128)(2,1)}, u32[]{:S(2)}) copy-start(bf16[592,4096]{1,0:T(8,128)(2,1)} %grad_ref.1) | copy-start | bytes 14548996

commit v2 on v1

v2 whole, which is shorter than its diff:
```python
import jax
import jax.numpy as jnp
from jax import lax
from jax.experimental import pallas as pl
from jax.experimental.pallas import tpu as pltpu
from jax.sharding import PartitionSpec as P

NY = 8
NZ = 8
NT = 4
TOKENS = 148
STEP = 144
SLOT = 160
DEPTH = 592
ROWS = 256
HALF = 128
HID = 4096
GROUP = 2048
EPS = 1e-06
F32 = jnp.float32
BF16 = jnp.bfloat16
MESH = pl.DeviceIdType.MESH
FAR_FIRST = (4, 3, 5, 2, 6, 1, 7)
TARGETS = (-4, -3, 3, -1, 1, 2, -2)
HOPS = (-2, -1, 1, -1, 1, 2, -2)


def row_order(group):
    new = lax.broadcasted_iota(jnp.int32, (ROWS, ROWS), 0)
    old = lax.broadcasted_iota(jnp.int32, (ROWS, ROWS), 1)
    core, first, second, i = new >> 7, (new >> 4) & 7, (new >> 1) & 7, new & 1
    y, z = (first, second) if group == 0 else (second, first)
    return jnp.where(old == 32 * y + 4 * z + 2 * core + i, 1.0, 0.0).astype(BF16)


def hadamard_pair():
    row = lax.broadcasted_iota(jnp.int32, (256, 256), 0)
    column = lax.broadcasted_iota(jnp.int32, (256, 256), 1)
    both = row & column & 127
    both = both ^ (both >> 4)
    both = both ^ (both >> 2)
    both = both ^ (both >> 1)
    sign = jnp.where((both & 1) == 0, 0.0625, -0.0625)
    return jnp.where((row >> 7) == (column >> 7), sign, 0.0).astype(BF16)


def kernel(
    tok_ref, grad_ref, dec_ref, tot_ref,
    shifted, table, slots, gbuf, turned, part, rot, other, squares,
    qall, qfirst, q1, q2, peak, inv, code, land1, acc, w, pack, land2,
    gsem, tsend, trecv, q1send, q1recv, q2send, q2recv, xsend, xrecv,
    send1, recv1, send2, recv2,
):
    dp = lax.axis_index("dp")
    t = lax.axis_index("tensor")
    c = lax.rem(dp, 2)
    z = lax.rem(lax.div(dp, 2), NZ)
    y = lax.div(dp, 2 * NZ)
    oc = 1 - c

    def device(yy, zz, cc):
        return (yy * (2 * NZ) + zz * 2 + cc, t)

    def shift(value, k, n):
        return lax.rem(value + k, n)

    barrier = pltpu.get_barrier_semaphore()
    peers_t = [(dp, shift(t, k, NT)) for k in range(1, NT)]
    peers_1 = [
        (kz * 2 + kc, shift(c, kc, 2), device(y, shift(z, kz, NZ), shift(c, kc, 2)))
        for kz in range(NZ)
        for kc in range(2)
        if kz + kc > 0
    ]
    peers_y = [device(shift(y, k, NY), z, c) for k in range(1, NY)]
    everyone = peers_t + [p[2] for p in peers_1] + peers_y
    for peer in everyone:
        pl.semaphore_signal(barrier, inc=1, device_id=peer, device_id_type=MESH)
    grad_copy = pltpu.make_async_copy(grad_ref, gbuf, gsem)
    grad_copy.start()
    table[...] = hadamard_pair()
    shifted[...] = jnp.zeros((SLOT, ROWS), F32)
    shifted[0:TOKENS, :] = tok_ref[...].astype(F32)
    slots[0] = pltpu.roll(shifted[...], 4 * t, 0).astype(BF16)
    pl.semaphore_wait(barrier, len(everyone))

    def tokens(k):
        return pltpu.make_async_remote_copy(
            src_ref=slots.at[0], dst_ref=slots.at[k],
            send_sem=tsend.at[k], recv_sem=trecv.at[k],
            device_id=(dp, shift(t, k, NT)), device_id_type=MESH,
        )

    for k in (1, 3, 2):
        tokens(k).start()
    squares[...] = jnp.zeros_like(squares)
    for k in (0, 1, 3, 2):
        source = shift(t, NT - k, NT)
        if k > 0:
            tokens(k).wait_recv()
        features = slots[k]
        for g in range(2):
            turned[g] = lax.dot_general(
                row_order(g), features, (((1,), (1,)), ((), ())), preferred_element_type=F32
            ).astype(BF16)
        if k == 0:
            grad_copy.wait()
        depth = pl.ds(pl.multiple_of(source * STEP, 16), SLOT)

        def columns(n, carry):
            g = lax.div(n, 2)
            left = turned[g]
            for tile in range(4):
                at = pl.ds(pl.multiple_of(n * 1024 + tile * 256, 256), 256)
                value = jnp.dot(left, gbuf[depth, at], preferred_element_type=F32)
                if k > 0:
                    value = part[:, at] + value
                part[:, at] = value
                if k == 2:
                    both = value * value
                    squares[g] = squares[g] + (both[:, :128] + both[:, 128:])
            return carry

        lax.fori_loop(0, 4, columns, 0)
    ones = jnp.ones((8, 128), F32)
    for g in range(2):
        q = lax.dot_general(
            ones, squares[g], (((1,), (1,)), ((), ())),
            preferred_element_type=F32, precision=lax.Precision.HIGHEST,
        )
        for half in range(2):
            qall[half, g:g + 1, :] = q[0:1, half * HALF:(half + 1) * HALF]

    for slot, core, peer in peers_1:
        pltpu.make_async_remote_copy(
            src_ref=qall.at[core], dst_ref=q1.at[slot],
            send_sem=q1send, recv_sem=q1recv, device_id=peer, device_id_type=MESH,
        ).start()

    def rotate(half, n):
        g, j = lax.div(n, 2), lax.rem(n, 2)
        rows = pl.ds(pl.multiple_of(half * HALF, HALF), HALF)
        value = jnp.concatenate(
            [
                part[rows, pl.ds(pl.multiple_of(n * 1024 + m * 256, 256), 256)]
                for m in range(4)
            ],
            axis=0,
        )
        high = value.astype(BF16)
        low = (value - high.astype(F32)).astype(BF16)
        result = (
            jnp.dot(high, table[...], preferred_element_type=F32)
            + jnp.dot(low, table[...], preferred_element_type=F32)
        ).astype(BF16)
        for m in range(4):
            at = pl.ds(pl.multiple_of(j * 1024 + m * 256, 256), 256)
            rot[g, rows, at] = result[m * HALF:(m + 1) * HALF]

    def cross(n):
        g, at = lax.div(n, 2), pl.ds(pl.multiple_of(lax.rem(n, 2) * 1024, 1024), 1024)
        return pltpu.make_async_remote_copy(
            src_ref=rot.at[g, pl.ds(pl.multiple_of(oc * HALF, HALF), HALF), at],
            dst_ref=other.at[g, :, at],
            send_sem=xsend.at[n], recv_sem=xrecv.at[n],
            device_id=device(y, z, oc), device_id_type=MESH,
        )

    def rotate_theirs(n, carry):
        rotate(oc, n)
        cross(n).start()
        return carry

    def rotate_mine(n, carry):
        rotate(c, n)
        return carry

    lax.fori_loop(0, 4, rotate_theirs, 0)

    q1_all = pltpu.make_async_remote_copy(
        src_ref=q1.at[pl.ds(1, 15)], dst_ref=q1.at[pl.ds(1, 15)],
        send_sem=q1send, recv_sem=q1recv, device_id=device(y, z, oc), device_id_type=MESH,
    )
    q1_all.wait_recv()
    best = qall[c]
    for slot in range(1, 16):
        best = jnp.maximum(best, q1[slot])
    qfirst[...] = best
    for k in range(1, NY):
        pltpu.make_async_remote_copy(
            src_ref=qfirst, dst_ref=q2.at[k],
            send_sem=q2send, recv_sem=q2recv, device_id=peers_y[k - 1], device_id_type=MESH,
        ).start()
    lax.fori_loop(0, 4, rotate_mine, 0)
    q2_all = pltpu.make_async_remote_copy(
        src_ref=q2.at[pl.ds(1, 7)], dst_ref=q2.at[pl.ds(1, 7)],
        send_sem=q2send, recv_sem=q2recv, device_id=peers_y[0], device_id_type=MESH,
    )
    q2_all.wait_recv()
    best = qfirst[...]
    for k in range(1, NY):
        best = jnp.maximum(best, q2[k])
    best = jnp.sqrt(best / float(GROUP) + EPS)
    for g in range(2):
        wide = jnp.transpose(jnp.broadcast_to(best[g:g + 1, :], (HALF, 128)))
        peak[g] = wide
        inv[g] = 0.7071067811865476 / wide
    for n in range(4):
        cross(n).wait_recv()

    side = 1 - 2 * c

    def away(g, k):
        return lax.rem(y + g * (z - y) + 8 + side * k, 8)

    def coded(g, k):
        place = away(g, k)
        rows = pl.ds(pl.multiple_of(place * 16, 16), 16)
        mine = pl.ds(pl.multiple_of(c * HALF + place * 16, 16), 16)
        scale = jnp.concatenate([inv[g, rows, :]] * (GROUP // 128), axis=1)
        own = jnp.clip(rot[g, mine, :].astype(F32) * scale, -1.0, 1.0)
        return own + jnp.clip(other[g, rows, :].astype(F32) * scale, -1.0, 1.0)

    def first(g, n):
        hop = away(g, HOPS[n]) - away(g, 0)
        peer = (dp + hop * (2 * NZ - 14 * g), t)
        return pltpu.make_async_remote_copy(
            src_ref=code.at[g, n], dst_ref=land1.at[g, n],
            send_sem=send1.at[g, n], recv_sem=recv1.at[g, n],
            device_id=peer, device_id_type=MESH,
        )

    def send_first(g, carry):
        for n in (0, 1, 2):
            code[g, n] = coded(g, TARGETS[n]).astype(BF16)
            first(g, n).start()
        return carry

    def send_direct(g, carry):
        for n in (3, 4):
            code[g, n] = coded(g, TARGETS[n]).astype(BF16)
            first(g, n).start()
        return carry

    def relay(g, carry):
        for n, parts in ((5, (2,)), (6, (1, 0))):
            value = coded(g, TARGETS[n])
            for part_n in parts:
                first(g, part_n).wait_recv()
                value = value + land1[g, part_n].astype(F32)
            code[g, n] = value.astype(BF16)
            first(g, n).start()
        return carry

    def keep(g, carry):
        acc[g] = coded(g, 0)
        return carry

    for step in (send_first, send_direct, relay, keep):
        lax.fori_loop(0, 2, step, 0)

    def second(g, k):
        peer = device(y, shift(z, k, NZ), c) if g == 0 else device(shift(y, k, NY), z, c)
        return pltpu.make_async_remote_copy(
            src_ref=pack.at[g, shift((z, y)[g], k, 8)], dst_ref=land2.at[g, k],
            send_sem=send2.at[g, k], recv_sem=recv2.at[g, k],
            device_id=peer, device_id_type=MESH,
        )

    for n in (3, 4, 5, 6):
        for g in range(2):
            first(g, n).wait_recv()
            acc[g] = acc[g] + land1[g, n].astype(F32)
    for g in range(2):
        for block in range(16):
            w[g, block * 16:(block + 1) * 16, :] = acc[g, :, block * 128:(block + 1) * 128]
        for place in range(8):
            pack[g, place] = jnp.concatenate(
                [w[g, pl.ds(place * 2 + i, 16, stride=16), :] for i in range(2)], axis=0
            ).astype(BF16)
        for k in FAR_FIRST:
            second(g, k).start()

    for g in range(2):
        total = pack[g, (z, y)[g]].astype(F32)
        for k in FAR_FIRST:
            second(g, k).wait_recv()
            total = total + land2[g, k].astype(F32)
        for i in range(2):
            row = (y, z)[g] * 16 + (z, y)[g] * 2 + i
            value = total[i * 16:(i + 1) * 16]
            at = i * 32 + g * 16
            tot_ref[at:at + 16, :] = value
            dec_ref[at:at + 16, :] = value * (2.0 * peak[g, pl.ds(row, 1), :])

    for k in range(1, NT):
        tokens(k).wait_send()
    q1_all.wait_send()
    q2_all.wait_send()
    for g in range(2):
        for n in range(2):
            cross(2 * g + n).wait_send()
        for n in range(7):
            first(g, n).wait_send()
        for k in FAR_FIRST:
            second(g, k).wait_send()


def local(tokens_in, grad_hidden):
    dma = pltpu.SemaphoreType.DMA
    decoded, total = pl.pallas_call(
        kernel,
        out_shape=[jax.ShapeDtypeStruct((64, 128), F32)] * 2,
        in_specs=[
            pl.BlockSpec(memory_space=pltpu.VMEM),
            pl.BlockSpec(memory_space=pl.ANY),
        ],
        out_specs=[pl.BlockSpec(memory_space=pltpu.VMEM)] * 2,
        scratch_shapes=[
            pltpu.VMEM((SLOT, ROWS), F32),
            pltpu.VMEM((256, 256), BF16),
            pltpu.VMEM((NT, SLOT, ROWS), BF16),
            pltpu.VMEM((DEPTH, HID), BF16),
            pltpu.VMEM((2, ROWS, SLOT), BF16),
            pltpu.VMEM((ROWS, HID), F32),
            pltpu.VMEM((2, ROWS, GROUP), BF16),
            pltpu.VMEM((2, HALF, GROUP), BF16),
            pltpu.VMEM((2, ROWS, 128), F32),
            pltpu.VMEM((2, 2, 128), F32),
            pltpu.VMEM((2, 128), F32),
            pltpu.VMEM((16, 2, 128), F32),
            pltpu.VMEM((8, 2, 128), F32),
            pltpu.VMEM((2, HALF, 128), F32),
            pltpu.VMEM((2, HALF, 128), F32),
            pltpu.VMEM((2, 7, 16, GROUP), BF16),
            pltpu.VMEM((2, 7, 16, GROUP), BF16),
            pltpu.VMEM((2, 16, GROUP), F32),
            pltpu.VMEM((2, 256, 128), F32),
            pltpu.VMEM((2, 8, 32, 128), BF16),
            pltpu.VMEM((2, 8, 32, 128), BF16),
            dma, dma((NT,)), dma((NT,)), dma, dma, dma, dma, dma((4,)), dma((4,)),
            dma((2, 7)), dma((2, 7)), dma((2, 8)), dma((2, 8)),
        ],
        compiler_params=pltpu.CompilerParams(
            collective_id=0, has_side_effects=True, vmem_limit_bytes=53 * 1024 * 1024
        ),
        cost_estimate=pl.CostEstimate(
            flops=2 * DEPTH * ROWS * HID, bytes_accessed=2 * DEPTH * HID, transcendentals=0
        ),
    )(tokens_in, grad_hidden)
    return decoded.reshape(2, HID), total.reshape(2, HID)


def solution(mesh):
    placed = (P(("dp", "tensor"), None), P("dp", "tensor"))
    return jax.shard_map(
        local,
        mesh=mesh,
        in_specs=placed,
        out_specs=(P("dp", "tensor"), P("dp", "tensor")),
        check_vma=False,
    )
```

time: 57.5 us -> 53.5 us (0.930)
  the two profiles are of different devices: /device:TPU:1 before, /device:TPU:8 now
where the time goes in v2:
time: 53.5 us; the launch traced here: 53.3 us
  Pallas kernels  50.5 us (94%)
  local copies, waits for them, and re-layouts  2.15 us (4%)
  between operations  0.65 us (1%)
    pallas_call x1, Pallas kernels, local(): pl.pallas_call(kernel, out_shape=[jax.ShapeDtypeStruct((64, 128), F32)] *...  50.5 us
    reshape x2, local copies, waits for them, and re-layouts, local(): return (decoded.reshape(2, HID), total.reshape(2, HID))  1.27 us

profile of v2, /device:TPU:8, one launch (start us, length us, event | category | flops | bytes accessed | tf_op | source)
XLA Modules:
  0.0 53.3 jit_solution(5028473880907905323)
XLA Ops:
  0.6 0.0 copy-start
  0.6 0.9 %copy-done = bf16[148,256]{1,0:T(8,128)(2,1)S(1)} copy-done((bf16[148,256]{1,0:T(8,128)(2,1)S(1)}, bf16[148,256]{1,0:T(8,128)(2,1)}, u32[]{:S(2)}) %copy-start) | copy-done | bytes 75800
  1.5 50.5 %shard_map.41 = (f32[64,128]{1,0:T(8,128)S(1)}, f32[64,128]{1,0:T(8,128)S(1)}) custom-call(bf16[148,256]{1,0:T(8,128)(2,1)S(1)} %copy-done, bf16[592,4096]{1,0:T(8,128)(2,1)} %grad_ref.1), custom_call_target="tpu_custom_call" | custom-call | flops 1241513984 | bytes 4849664 | tf_op jit(solution)/shard_map/pallas_call | solution.py:311
  52.0 0.6 %reshape.10 = f32[2,4096]{1,0:T(2,128)} reshape(f32[64,128]{1,0:T(8,128)S(1)} %get-tuple-element.4) | data formatting | bytes 65536 | tf_op jit(solution)/shard_map/reshape | solution.py:351
  52.7 0.6 %reshape.11 = f32[2,4096]{1,0:T(2,128)} reshape(f32[64,128]{1,0:T(8,128)S(1)} %get-tuple-element.5) | data formatting | bytes 65536 | tf_op jit(solution)/shard_map/reshape | solution.py:351
Async XLA Ops:
  0.6 0.9 %copy-start = (bf16[148,256]{1,0:T(8,128)(2,1)S(1)}, bf16[148,256]{1,0:T(8,128)(2,1)}, u32[]{:S(2)}) copy-start(bf16[148,256]{1,0:T(8,128)(2,1)} %tok_ref.1) | copy-start | bytes 227332

commit v3 on v2

--- a/solution.py
+++ b/solution.py
@@ -21,8 +21,10 @@
 BF16 = jnp.bfloat16
 MESH = pl.DeviceIdType.MESH
 FAR_FIRST = (4, 3, 5, 2, 6, 1, 7)
-TARGETS = (-4, -3, 3, -1, 1, 2, -2)
-HOPS = (-2, -1, 1, -1, 1, 2, -2)
+RAW_TARGETS = (-4, -3, 3)
+RAW_HOPS = (-2, -1, 1)
+SUM_HOPS = (-2, 2, -1, 1)
+RAW_PARTS = ((0, 1), (2,), (), ())
 
 
 def row_order(group):
@@ -46,9 +48,9 @@
 
 def kernel(
     tok_ref, grad_ref, dec_ref, tot_ref,
-    shifted, table, slots, gbuf, turned, part, rot, other, squares,
-    qall, qfirst, q1, q2, peak, inv, code, land1, acc, w, pack, land2,
-    gsem, tsend, trecv, q1send, q1recv, q2send, q2recv, xsend, xrecv,
+    tok, shifted, order, table, slots, gbuf, turned, part, rot, other, squares,
+    qall, qfirst, q1, q2, inv, land0, code, land1, acc, w, pack, land2,
+    far, gsem, toksem, tsend, trecv, q1send, q1recv, q2send, q2recv, xsend, xrecv, send0, recv0,
     send1, recv1, send2, recv2,
 ):
     dp = lax.axis_index("dp")
@@ -73,16 +75,26 @@
         if kz + kc > 0
     ]
     peers_y = [device(shift(y, k, NY), z, c) for k in range(1, NY)]
-    everyone = peers_t + [p[2] for p in peers_1] + peers_y
-    for peer in everyone:
+
+    def along(g, k, core):
+        place = lax.rem(y + g * (z - y) + 8 + (1 - 2 * core) * k, 8)
+        return place, (dp + (place - y - g * (z - y)) * (2 * NZ - 14 * g) + core - c, t)
+
+    near = list(peers_t) + [(dp + oc - c, t)]
+    for g in range(2):
+        for k in (1, -1, 2, -2):
+            near += [along(g, k, c)[1], along(g, k, oc)[1]]
+    for peer in near:
         pl.semaphore_signal(barrier, inc=1, device_id=peer, device_id_type=MESH)
+    tok_copy = pltpu.make_async_copy(tok_ref, tok, toksem)
+    tok_copy.start()
     grad_copy = pltpu.make_async_copy(grad_ref, gbuf, gsem)
     grad_copy.start()
-    table[...] = hadamard_pair()
     shifted[...] = jnp.zeros((SLOT, ROWS), F32)
-    shifted[0:TOKENS, :] = tok_ref[...].astype(F32)
+    tok_copy.wait()
+    shifted[0:TOKENS, :] = tok[...].astype(F32)
     slots[0] = pltpu.roll(shifted[...], 4 * t, 0).astype(BF16)
-    pl.semaphore_wait(barrier, len(everyone))
+    pl.semaphore_wait(barrier, len(near))
 
     def tokens(k):
         return pltpu.make_async_remote_copy(
@@ -93,6 +105,14 @@
 
     for k in (1, 3, 2):
         tokens(k).start()
+    for g in range(2):
+        for k in (2, -2):
+            pl.semaphore_signal(
+                far, inc=1, device_id=along(g, k, c)[1], device_id_type=MESH
+            )
+    for g in range(2):
+        order[g] = row_order(g)
+    table[...] = hadamard_pair()
     squares[...] = jnp.zeros_like(squares)
     for k in (0, 1, 3, 2):
         source = shift(t, NT - k, NT)
@@ -101,7 +121,7 @@
         features = slots[k]
         for g in range(2):
             turned[g] = lax.dot_general(
-                row_order(g), features, (((1,), (1,)), ((), ())), preferred_element_type=F32
+                order[g], features, (((1,), (1,)), ((), ())), preferred_element_type=F32
             ).astype(BF16)
         if k == 0:
             grad_copy.wait()
@@ -131,6 +151,8 @@
         for half in range(2):
             qall[half, g:g + 1, :] = q[0:1, half * HALF:(half + 1) * HALF]
 
+    pl.semaphore_wait(far, 4)
+
     for slot, core, peer in peers_1:
         pltpu.make_async_remote_copy(
             src_ref=qall.at[core], dst_ref=q1.at[slot],
@@ -166,16 +188,33 @@
             device_id=device(y, z, oc), device_id_type=MESH,
         )
 
-    def rotate_theirs(n, carry):
-        rotate(oc, n)
-        cross(n).start()
+    def raw(g, other_core, j):
+        core = shift(c, other_core, 2)
+        place = along(g, RAW_TARGETS[j], core)[0]
+        rows = pl.ds(pl.multiple_of(core * HALF + place * 16, 16), 16)
+        n = other_core * 3 + j
+        return pltpu.make_async_remote_copy(
+            src_ref=rot.at[g, rows, :], dst_ref=land0.at[g, n],
+            send_sem=send0.at[g, n], recv_sem=recv0.at[g, n],
+            device_id=along(g, RAW_HOPS[j], core)[1], device_id_type=MESH,
+        )
+
+    def rotate_theirs(g, carry):
+        for j in range(2):
+            rotate(oc, 2 * g + j)
+            cross(2 * g + j).start()
+        for j in range(3):
+            raw(g, 1, j).start()
         return carry
 
-    def rotate_mine(n, carry):
-        rotate(c, n)
+    def rotate_mine(g, carry):
+        for j in range(2):
+            rotate(c, 2 * g + j)
+        for j in range(3):
+            raw(g, 0, j).start()
         return carry
 
-    lax.fori_loop(0, 4, rotate_theirs, 0)
+    lax.fori_loop(0, 2, rotate_theirs, 0)
 
     q1_all = pltpu.make_async_remote_copy(
         src_ref=q1.at[pl.ds(1, 15)], dst_ref=q1.at[pl.ds(1, 15)],
@@ -191,7 +230,7 @@
             src_ref=qfirst, dst_ref=q2.at[k],
             send_sem=q2send, recv_sem=q2recv, device_id=peers_y[k - 1], device_id_type=MESH,
         ).start()
-    lax.fori_loop(0, 4, rotate_mine, 0)
+    lax.fori_loop(0, 2, rotate_mine, 0)
     q2_all = pltpu.make_async_remote_copy(
         src_ref=q2.at[pl.ds(1, 7)], dst_ref=q2.at[pl.ds(1, 7)],
         send_sem=q2send, recv_sem=q2recv, device_id=peers_y[0], device_id_type=MESH,
@@ -200,64 +239,47 @@
     best = qfirst[...]
     for k in range(1, NY):
         best = jnp.maximum(best, q2[k])
-    best = jnp.sqrt(best / float(GROUP) + EPS)
-    for g in range(2):
-        wide = jnp.transpose(jnp.broadcast_to(best[g:g + 1, :], (HALF, 128)))
-        peak[g] = wide
-        inv[g] = 0.7071067811865476 / wide
+    best = 0.7071067811865476 / jnp.sqrt(best / float(GROUP) + EPS)
+    for g in range(2):
+        inv[g] = jnp.transpose(jnp.broadcast_to(best[g:g + 1, :], (HALF, 128)))
     for n in range(4):
         cross(n).wait_recv()
 
-    side = 1 - 2 * c
-
-    def away(g, k):
-        return lax.rem(y + g * (z - y) + 8 + side * k, 8)
-
-    def coded(g, k):
-        place = away(g, k)
+    def coded(g, k, parts):
+        place = along(g, k, c)[0]
         rows = pl.ds(pl.multiple_of(place * 16, 16), 16)
         mine = pl.ds(pl.multiple_of(c * HALF + place * 16, 16), 16)
         scale = jnp.concatenate([inv[g, rows, :]] * (GROUP // 128), axis=1)
-        own = jnp.clip(rot[g, mine, :].astype(F32) * scale, -1.0, 1.0)
-        return own + jnp.clip(other[g, rows, :].astype(F32) * scale, -1.0, 1.0)
+        value = jnp.clip(rot[g, mine, :].astype(F32) * scale, -1.0, 1.0)
+        value = value + jnp.clip(other[g, rows, :].astype(F32) * scale, -1.0, 1.0)
+        for j in parts:
+            for n in (j, 3 + j):
+                value = value + jnp.clip(land0[g, n].astype(F32) * scale, -1.0, 1.0)
+        return value
 
     def first(g, n):
-        hop = away(g, HOPS[n]) - away(g, 0)
-        peer = (dp + hop * (2 * NZ - 14 * g), t)
         return pltpu.make_async_remote_copy(
             src_ref=code.at[g, n], dst_ref=land1.at[g, n],
             send_sem=send1.at[g, n], recv_sem=recv1.at[g, n],
-            device_id=peer, device_id_type=MESH,
-        )
-
-    def send_first(g, carry):
-        for n in (0, 1, 2):
-            code[g, n] = coded(g, TARGETS[n]).astype(BF16)
+            device_id=along(g, SUM_HOPS[n], c)[1], device_id_type=MESH,
+        )
+
+    for n in range(4):
+        def send_sum(g, carry, n=n):
+            for j in RAW_PARTS[n]:
+                for other_core in range(2):
+                    raw(g, other_core, j).wait_recv()
+            code[g, n] = coded(g, SUM_HOPS[n], RAW_PARTS[n]).astype(BF16)
             first(g, n).start()
+            return carry
+
+        lax.fori_loop(0, 2, send_sum, 0)
+
+    def keep(g, carry):
+        acc[g] = coded(g, 0, ())
         return carry
 
-    def send_direct(g, carry):
-        for n in (3, 4):
-            code[g, n] = coded(g, TARGETS[n]).astype(BF16)
-            first(g, n).start()
-        return carry
-
-    def relay(g, carry):
-        for n, parts in ((5, (2,)), (6, (1, 0))):
-            value = coded(g, TARGETS[n])
-            for part_n in parts:
-                first(g, part_n).wait_recv()
-                value = value + land1[g, part_n].astype(F32)
-            code[g, n] = value.astype(BF16)
-            first(g, n).start()
-        return carry
-
-    def keep(g, carry):
-        acc[g] = coded(g, 0)
-        return carry
-
-    for step in (send_first, send_direct, relay, keep):
-        lax.fori_loop(0, 2, step, 0)
+    lax.fori_loop(0, 2, keep, 0)
 
     def second(g, k):
         peer = device(y, shift(z, k, NZ), c) if g == 0 else device(shift(y, k, NY), z, c)
@@ -267,11 +289,12 @@
             device_id=peer, device_id_type=MESH,
         )
 
-    for n in (3, 4, 5, 6):
-        for g in range(2):
+    for g in range(2):
+        value = acc[g]
+        for n in (2, 3, 1, 0):
             first(g, n).wait_recv()
-            acc[g] = acc[g] + land1[g, n].astype(F32)
-    for g in range(2):
+            value = value + land1[g, n].astype(F32)
+        acc[g] = value
         for block in range(16):
             w[g, block * 16:(block + 1) * 16, :] = acc[g, :, block * 128:(block + 1) * 128]
         for place in range(8):
@@ -289,9 +312,10 @@
         for i in range(2):
             row = (y, z)[g] * 16 + (z, y)[g] * 2 + i
             value = total[i * 16:(i + 1) * 16]
-            at = i * 32 + g * 16
-            tot_ref[at:at + 16, :] = value
-            dec_ref[at:at + 16, :] = value * (2.0 * peak[g, pl.ds(row, 1), :])
+            at = g * 16
+            scale = 1.4142135623730951 / inv[g, pl.ds(row, 1), :]
+            tot_ref[at:at + 16, i, :] = value
+            dec_ref[at:at + 16, i, :] = value * scale
 
     for k in range(1, NT):
         tokens(k).wait_send()
@@ -300,7 +324,10 @@
     for g in range(2):
         for n in range(2):
             cross(2 * g + n).wait_send()
-        for n in range(7):
+        for j in range(3):
+            raw(g, 0, j).wait_send()
+            raw(g, 1, j).wait_send()
+        for n in range(4):
             first(g, n).wait_send()
         for k in FAR_FIRST:
             second(g, k).wait_send()
@@ -310,14 +337,13 @@
     dma = pltpu.SemaphoreType.DMA
     decoded, total = pl.pallas_call(
         kernel,
-        out_shape=[jax.ShapeDtypeStruct((64, 128), F32)] * 2,
-        in_specs=[
-            pl.BlockSpec(memory_space=pltpu.VMEM),
-            pl.BlockSpec(memory_space=pl.ANY),
-        ],
+        out_shape=[jax.ShapeDtypeStruct((32, 2, 128), F32)] * 2,
+        in_specs=[pl.BlockSpec(memory_space=pl.ANY)] * 2,
         out_specs=[pl.BlockSpec(memory_space=pltpu.VMEM)] * 2,
         scratch_shapes=[
+            pltpu.VMEM((TOKENS, ROWS), BF16),
             pltpu.VMEM((SLOT, ROWS), F32),
+            pltpu.VMEM((2, 256, 256), BF16),
             pltpu.VMEM((256, 256), BF16),
             pltpu.VMEM((NT, SLOT, ROWS), BF16),
             pltpu.VMEM((DEPTH, HID), BF16),
@@ -331,24 +357,26 @@
             pltpu.VMEM((16, 2, 128), F32),
             pltpu.VMEM((8, 2, 128), F32),
             pltpu.VMEM((2, HALF, 128), F32),
-            pltpu.VMEM((2, HALF, 128), F32),
-            pltpu.VMEM((2, 7, 16, GROUP), BF16),
-            pltpu.VMEM((2, 7, 16, GROUP), BF16),
+            pltpu.VMEM((2, 6, 16, GROUP), BF16),
+            pltpu.VMEM((2, 4, 16, GROUP), BF16),
+            pltpu.VMEM((2, 4, 16, GROUP), BF16),
             pltpu.VMEM((2, 16, GROUP), F32),
             pltpu.VMEM((2, 256, 128), F32),
             pltpu.VMEM((2, 8, 32, 128), BF16),
             pltpu.VMEM((2, 8, 32, 128), BF16),
-            dma, dma((NT,)), dma((NT,)), dma, dma, dma, dma, dma((4,)), dma((4,)),
-            dma((2, 7)), dma((2, 7)), dma((2, 8)), dma((2, 8)),
+            pltpu.SemaphoreType.REGULAR, dma, dma, dma((NT,)), dma((NT,)), dma, dma, dma, dma, dma((4,)), dma((4,)),
+            dma((2, 6)), dma((2, 6)), dma((2, 4)), dma((2, 4)), dma((2, 8)), dma((2, 8)),
         ],
         compiler_params=pltpu.CompilerParams(
-            collective_id=0, has_side_effects=True, vmem_limit_bytes=53 * 1024 * 1024
+            collective_id=0, has_side_effects=True, vmem_limit_bytes=int(53.85 * 1024 * 1024)
         ),
         cost_estimate=pl.CostEstimate(
             flops=2 * DEPTH * ROWS * HID, bytes_accessed=2 * DEPTH * HID, transcendentals=0
         ),
     )(tokens_in, grad_hidden)
-    return decoded.reshape(2, HID), total.reshape(2, HID)
+    return tuple(
+        jnp.transpose(value, (1, 0, 2)).reshape(2, HID) for value in (decoded, total)
+    )
 
 
 def solution(mesh):

time: 53.5 us -> 48.6 us (0.908)
  the two profiles are of different devices: /device:TPU:8 before, /device:TPU:1 now
where the time goes in v3:
time: 48.6 us; the launch traced here: 48.4 us
  Pallas kernels  46.6 us (96%)
  local copies, waits for them, and re-layouts  1.23 us (3%)
  between operations  0.64 us (1%)
    pallas_call x1, Pallas kernels, local(): pl.pallas_call(kernel, out_shape=[jax.ShapeDtypeStruct((32, 2, 128), F32)...  46.6 us
    unnamed x2, local copies, waits for them, and re-layouts  1.23 us

profile of v3, /device:TPU:1, one launch (start us, length us, event | category | flops | bytes accessed | tf_op | source)
XLA Modules:
  0.0 48.4 jit_solution(8696889000558579821)
XLA Ops:
  0.6 46.6 %shard_map.41 = (f32[32,2,128]{2,1,0:T(2,128)S(1)}, f32[32,2,128]{2,1,0:T(2,128)S(1)}) custom-call(bf16[148,256]{1,0:T(8,128)(2,1)} %tok_ref.1, bf16[592,4096]{1,0:T(8,128)(2,1)} %grad_ref.1), custom_call_target="tpu_custom_call" | custom-call | flops 1241513984 | bytes 4849664 | tf_op jit(solution)/shard_map/pallas_call | solution.py:338
  47.2 0.6 %copy.6 = f32[2,4096]{1,0:T(2,128)} copy(f32[2,4096]{1,0:T(2,128)S(1)} %bitcast.7) | data formatting | bytes 65536
  47.8 0.6 %copy.7 = f32[2,4096]{1,0:T(2,128)} copy(f32[2,4096]{1,0:T(2,128)S(1)} %bitcast.6) | data formatting | bytes 65536

commit v4 on v3

--- a/solution.py
+++ b/solution.py
@@ -47,7 +47,7 @@
 
 
 def kernel(
-    tok_ref, grad_ref, dec_ref, tot_ref,
+    tok_ref, grad_ref, out_ref,
     tok, shifted, order, table, slots, gbuf, turned, part, rot, other, squares,
     qall, qfirst, q1, q2, inv, land0, code, land1, acc, w, pack, land2,
     far, gsem, toksem, tsend, trecv, q1send, q1recv, q2send, q2recv, xsend, xrecv, send0, recv0,
@@ -67,7 +67,7 @@
         return lax.rem(value + k, n)
 
     barrier = pltpu.get_barrier_semaphore()
-    peers_t = [(dp, shift(t, k, NT)) for k in range(1, NT)]
+    peers_t = [(dp, shift(t, k, NT)) for k in (1, 3)]
     peers_1 = [
         (kz * 2 + kc, shift(c, kc, 2), device(y, shift(z, kz, NZ), shift(c, kc, 2)))
         for kz in range(NZ)
@@ -103,7 +103,15 @@
             device_id=(dp, shift(t, k, NT)), device_id_type=MESH,
         )
 
-    for k in (1, 3, 2):
+    def pass_on(k):
+        rows = pl.ds(0 if k == 1 else SLOT // 2, SLOT // 2)
+        return pltpu.make_async_remote_copy(
+            src_ref=slots.at[k, rows], dst_ref=slots.at[2, rows],
+            send_sem=tsend.at[k - 1], recv_sem=trecv.at[k - 1],
+            device_id=(dp, shift(t, k, NT)), device_id_type=MESH,
+        )
+
+    for k in (1, 3):
         tokens(k).start()
     for g in range(2):
         for k in (2, -2):
@@ -116,8 +124,13 @@
     squares[...] = jnp.zeros_like(squares)
     for k in (0, 1, 3, 2):
         source = shift(t, NT - k, NT)
-        if k > 0:
-            tokens(k).wait_recv()
+        if k == 1:
+            for n in (1, 3):
+                tokens(n).wait_recv()
+                pass_on(n).start()
+        if k == 2:
+            for n in (1, 3):
+                pass_on(n).wait_recv()
         features = slots[k]
         for g in range(2):
             turned[g] = lax.dot_general(
@@ -215,6 +228,7 @@
         return carry
 
     lax.fori_loop(0, 2, rotate_theirs, 0)
+    lax.fori_loop(0, 2, rotate_mine, 0)
 
     q1_all = pltpu.make_async_remote_copy(
         src_ref=q1.at[pl.ds(1, 15)], dst_ref=q1.at[pl.ds(1, 15)],
@@ -230,7 +244,6 @@
             src_ref=qfirst, dst_ref=q2.at[k],
             send_sem=q2send, recv_sem=q2recv, device_id=peers_y[k - 1], device_id_type=MESH,
         ).start()
-    lax.fori_loop(0, 2, rotate_mine, 0)
     q2_all = pltpu.make_async_remote_copy(
         src_ref=q2.at[pl.ds(1, 7)], dst_ref=q2.at[pl.ds(1, 7)],
         send_sem=q2send, recv_sem=q2recv, device_id=peers_y[0], device_id_type=MESH,
@@ -314,11 +327,12 @@
             value = total[i * 16:(i + 1) * 16]
             at = g * 16
             scale = 1.4142135623730951 / inv[g, pl.ds(row, 1), :]
-            tot_ref[at:at + 16, i, :] = value
-            dec_ref[at:at + 16, i, :] = value * scale
-
-    for k in range(1, NT):
+            out_ref[1, at:at + 16, i, :] = value
+            out_ref[0, at:at + 16, i, :] = value * scale
+
+    for k in (1, 3):
         tokens(k).wait_send()
+        pass_on(k).wait_send()
     q1_all.wait_send()
     q2_all.wait_send()
     for g in range(2):
@@ -335,11 +349,11 @@
 
 def local(tokens_in, grad_hidden):
     dma = pltpu.SemaphoreType.DMA
-    decoded, total = pl.pallas_call(
+    result = pl.pallas_call(
         kernel,
-        out_shape=[jax.ShapeDtypeStruct((32, 2, 128), F32)] * 2,
+        out_shape=jax.ShapeDtypeStruct((2, 32, 2, 128), F32),
         in_specs=[pl.BlockSpec(memory_space=pl.ANY)] * 2,
-        out_specs=[pl.BlockSpec(memory_space=pltpu.VMEM)] * 2,
+        out_specs=pl.BlockSpec(memory_space=pltpu.VMEM),
         scratch_shapes=[
             pltpu.VMEM((TOKENS, ROWS), BF16),
             pltpu.VMEM((SLOT, ROWS), F32),
@@ -374,9 +388,8 @@
             flops=2 * DEPTH * ROWS * HID, bytes_accessed=2 * DEPTH * HID, transcendentals=0
         ),
     )(tokens_in, grad_hidden)
-    return tuple(
-        jnp.transpose(value, (1, 0, 2)).reshape(2, HID) for value in (decoded, total)
-    )
+    result = jnp.transpose(result, (0, 2, 1, 3)).reshape(2, 2, HID)
+    return result[0], result[1]
 
 
 def solution(mesh):

time: 48.6 us -> 46.9 us (0.965)
  Pallas kernels: 46.6 us -> 45.5 us
  local copies, waits for them, and re-layouts: 1.23 us -> 0.63 us
    unnamed x2 -> x0, local copies, waits for them, and re-layouts: 1.23 us -> none
    pallas_call x1, Pallas kernels: 46.6 us -> 45.5 us  [local(): pl.pallas_call(kernel, out_shape=jax.ShapeDtypeStruct((2, 32, 2, 128), F3...]
    squeeze x0 -> x1, local copies, waits for them, and re-layouts: none -> 0.63 us  [local(): return (result[0], result[1])]
where the time goes in v4:
time: 46.9 us; the launch traced here: 46.8 us
  Pallas kernels  45.5 us (97%)
  between operations  0.64 us (1%)
  local copies, waits for them, and re-layouts  0.63 us (1%)
    pallas_call x1, Pallas kernels, local(): pl.pallas_call(kernel, out_shape=jax.ShapeDtypeStruct((2, 32, 2, 128), F3...  45.5 us

profile of v4, /device:TPU:1, one launch (start us, length us, event | category | flops | bytes accessed | tf_op | source)
XLA Modules:
  0.0 46.8 jit_solution(17137416560063973761)
XLA Ops:
  0.6 45.5 %shard_map.41 = f32[2,32,2,128]{3,2,1,0:T(2,128)S(1)} custom-call(bf16[148,256]{1,0:T(8,128)(2,1)} %tok_ref.1, bf16[592,4096]{1,0:T(8,128)(2,1)} %grad_ref.1), custom_call_target="tpu_custom_call" | custom-call | flops 1241513984 | bytes 4849664 | tf_op jit(solution)/shard_map/pallas_call | solution.py:352
  46.2 0.6 %slice_bitcast_fusion = (f32[2,4096]{1,0:T(2,128)}, f32[2,4096]{1,0:T(2,128)}) fusion(f32[2,2,32,128]{3,1,2,0:T(2,128)S(1)} %bitcast.5), kind=kLoop, calls=%fused_computation | loop fusion | bytes 131072 | tf_op jit(solution)/shard_map/squeeze | solution.py:392

commit v5 on v4

--- a/solution.py
+++ b/solution.py
@@ -21,10 +21,11 @@
 BF16 = jnp.bfloat16
 MESH = pl.DeviceIdType.MESH
 FAR_FIRST = (4, 3, 5, 2, 6, 1, 7)
-RAW_TARGETS = (-4, -3, 3)
-RAW_HOPS = (-2, -1, 1)
-SUM_HOPS = (-2, 2, -1, 1)
-RAW_PARTS = ((0, 1), (2,), (), ())
+RAW_TARGETS = (-4, -3, 3, -1, 1)
+RAW_HOPS = (-2, -1, 1, -1, 1)
+SUM_HOPS = (-2, 2)
+RAW_PARTS = ((0, 1), (2,))
+OWN_PARTS = (3, 4)
 
 
 def row_order(group):
@@ -70,8 +71,8 @@
     peers_t = [(dp, shift(t, k, NT)) for k in (1, 3)]
     peers_1 = [
         (kz * 2 + kc, shift(c, kc, 2), device(y, shift(z, kz, NZ), shift(c, kc, 2)))
-        for kz in range(NZ)
-        for kc in range(2)
+        for kz in FAR_FIRST + (0,)
+        for kc in (1, 0)
         if kz + kc > 0
     ]
     peers_y = [device(shift(y, k, NY), z, c) for k in range(1, NY)]
@@ -121,44 +122,52 @@
     for g in range(2):
         order[g] = row_order(g)
     table[...] = hadamard_pair()
-    squares[...] = jnp.zeros_like(squares)
-    for k in (0, 1, 3, 2):
-        source = shift(t, NT - k, NT)
-        if k == 1:
-            for n in (1, 3):
-                tokens(n).wait_recv()
-                pass_on(n).start()
-        if k == 2:
-            for n in (1, 3):
-                pass_on(n).wait_recv()
-        features = slots[k]
-        for g in range(2):
-            turned[g] = lax.dot_general(
-                order[g], features, (((1,), (1,)), ((), ())), preferred_element_type=F32
-            ).astype(BF16)
-        if k == 0:
+    for step, ks in enumerate(((0,), (1, 3), (2,))):
+        if step == 1:
+            for k in ks:
+                tokens(k).wait_recv()
+                pass_on(k).start()
+        if step == 2:
+            for k in (1, 3):
+                pass_on(k).wait_recv()
+        for n, k in enumerate(ks):
+            features = slots[k]
+            for g in range(2):
+                turned[n, g] = lax.dot_general(
+                    order[g], features, (((1,), (1,)), ((), ())),
+                    preferred_element_type=F32,
+                ).astype(BF16)
+        if step == 0:
             grad_copy.wait()
-        depth = pl.ds(pl.multiple_of(source * STEP, 16), SLOT)
-
-        def columns(n, carry):
-            g = lax.div(n, 2)
-            left = turned[g]
+        depths = [
+            pl.ds(pl.multiple_of(shift(t, NT - k, NT) * STEP, 16), SLOT) for k in ks
+        ]
+
+        def columns(m, carry):
+            g = lax.div(m, 2)
+            total = None
             for tile in range(4):
-                at = pl.ds(pl.multiple_of(n * 1024 + tile * 256, 256), 256)
-                value = jnp.dot(left, gbuf[depth, at], preferred_element_type=F32)
-                if k > 0:
-                    value = part[:, at] + value
+                at = pl.ds(pl.multiple_of(m * 1024 + tile * 256, 256), 256)
+                value = part[:, at] if step > 0 else None
+                for n, depth in enumerate(depths):
+                    product = jnp.dot(
+                        turned[n, g], gbuf[depth, at], preferred_element_type=F32
+                    )
+                    value = product if value is None else value + product
                 part[:, at] = value
-                if k == 2:
+                if step == 2:
                     both = value * value
-                    squares[g] = squares[g] + (both[:, :128] + both[:, 128:])
+                    both = both[:, :128] + both[:, 128:]
+                    total = both if total is None else total + both
+            if step == 2:
+                squares[m] = total
             return carry
 
         lax.fori_loop(0, 4, columns, 0)
     ones = jnp.ones((8, 128), F32)
     for g in range(2):
         q = lax.dot_general(
-            ones, squares[g], (((1,), (1,)), ((), ())),
+            ones, squares[2 * g] + squares[2 * g + 1], (((1,), (1,)), ((), ())),
             preferred_element_type=F32, precision=lax.Precision.HIGHEST,
         )
         for half in range(2):
@@ -205,7 +214,7 @@
         core = shift(c, other_core, 2)
         place = along(g, RAW_TARGETS[j], core)[0]
         rows = pl.ds(pl.multiple_of(core * HALF + place * 16, 16), 16)
-        n = other_core * 3 + j
+        n = other_core * 5 + j
         return pltpu.make_async_remote_copy(
             src_ref=rot.at[g, rows, :], dst_ref=land0.at[g, n],
             send_sem=send0.at[g, n], recv_sem=recv0.at[g, n],
@@ -216,14 +225,14 @@
         for j in range(2):
             rotate(oc, 2 * g + j)
             cross(2 * g + j).start()
-        for j in range(3):
+        for j in range(5):
             raw(g, 1, j).start()
         return carry
 
     def rotate_mine(g, carry):
         for j in range(2):
             rotate(c, 2 * g + j)
-        for j in range(3):
+        for j in range(5):
             raw(g, 0, j).start()
         return carry
 
@@ -239,7 +248,7 @@
     for slot in range(1, 16):
         best = jnp.maximum(best, q1[slot])
     qfirst[...] = best
-    for k in range(1, NY):
+    for k in FAR_FIRST:
         pltpu.make_async_remote_copy(
             src_ref=qfirst, dst_ref=q2.at[k],
             send_sem=q2send, recv_sem=q2recv, device_id=peers_y[k - 1], device_id_type=MESH,
@@ -266,7 +275,7 @@
         value = jnp.clip(rot[g, mine, :].astype(F32) * scale, -1.0, 1.0)
         value = value + jnp.clip(other[g, rows, :].astype(F32) * scale, -1.0, 1.0)
         for j in parts:
-            for n in (j, 3 + j):
+            for n in (j, 5 + j):
                 value = value + jnp.clip(land0[g, n].astype(F32) * scale, -1.0, 1.0)
         return value
 
@@ -277,11 +286,14 @@
             device_id=along(g, SUM_HOPS[n], c)[1], device_id_type=MESH,
         )
 
-    for n in range(4):
+    def arrived(g, parts):
+        for j in parts:
+            for other_core in range(2):
+                raw(g, other_core, j).wait_recv()
+
+    for n in range(2):
         def send_sum(g, carry, n=n):
-            for j in RAW_PARTS[n]:
-                for other_core in range(2):
-                    raw(g, other_core, j).wait_recv()
+            arrived(g, RAW_PARTS[n])
             code[g, n] = coded(g, SUM_HOPS[n], RAW_PARTS[n]).astype(BF16)
             first(g, n).start()
             return carry
@@ -289,7 +301,8 @@
         lax.fori_loop(0, 2, send_sum, 0)
 
     def keep(g, carry):
-        acc[g] = coded(g, 0, ())
+        arrived(g, OWN_PARTS)
+        acc[g] = coded(g, 0, OWN_PARTS)
         return carry
 
     lax.fori_loop(0, 2, keep, 0)
@@ -304,7 +317,7 @@
 
     for g in range(2):
         value = acc[g]
-        for n in (2, 3, 1, 0):
+        for n in (1, 0):
             first(g, n).wait_recv()
             value = value + land1[g, n].astype(F32)
         acc[g] = value
@@ -338,10 +351,10 @@
     for g in range(2):
         for n in range(2):
             cross(2 * g + n).wait_send()
-        for j in range(3):
+        for j in range(5):
             raw(g, 0, j).wait_send()
             raw(g, 1, j).wait_send()
-        for n in range(4):
+        for n in range(2):
             first(g, n).wait_send()
         for k in FAR_FIRST:
             second(g, k).wait_send()
@@ -361,25 +374,25 @@
             pltpu.VMEM((256, 256), BF16),
             pltpu.VMEM((NT, SLOT, ROWS), BF16),
             pltpu.VMEM((DEPTH, HID), BF16),
-            pltpu.VMEM((2, ROWS, SLOT), BF16),
+            pltpu.VMEM((2, 2, ROWS, SLOT), BF16),
             pltpu.VMEM((ROWS, HID), F32),
             pltpu.VMEM((2, ROWS, GROUP), BF16),
             pltpu.VMEM((2, HALF, GROUP), BF16),
-            pltpu.VMEM((2, ROWS, 128), F32),
+            pltpu.VMEM((4, ROWS, 128), F32),
             pltpu.VMEM((2, 2, 128), F32),
             pltpu.VMEM((2, 128), F32),
             pltpu.VMEM((16, 2, 128), F32),
             pltpu.VMEM((8, 2, 128), F32),
             pltpu.VMEM((2, HALF, 128), F32),
-            pltpu.VMEM((2, 6, 16, GROUP), BF16),
-            pltpu.VMEM((2, 4, 16, GROUP), BF16),
-            pltpu.VMEM((2, 4, 16, GROUP), BF16),
+            pltpu.VMEM((2, 10, 16, GROUP), BF16),
+            pltpu.VMEM((2, 2, 16, GROUP), BF16),
+            pltpu.VMEM((2, 2, 16, GROUP), BF16),
             pltpu.VMEM((2, 16, GROUP), F32),
             pltpu.VMEM((2, 256, 128), F32),
             pltpu.VMEM((2, 8, 32, 128), BF16),
             pltpu.VMEM((2, 8, 32, 128), BF16),
             pltpu.SemaphoreType.REGULAR, dma, dma, dma((NT,)), dma((NT,)), dma, dma, dma, dma, dma((4,)), dma((4,)),
-            dma((2, 6)), dma((2, 6)), dma((2, 4)), dma((2, 4)), dma((2, 8)), dma((2, 8)),
+            dma((2, 10)), dma((2, 10)), dma((2, 2)), dma((2, 2)), dma((2, 8)), dma((2, 8)),
         ],
         compiler_params=pltpu.CompilerParams(
             collective_id=0, has_side_effects=True, vmem_limit_bytes=int(53.85 * 1024 * 1024)

time: 46.9 us -> 47.8 us (1.019)
  the two profiles are of different devices: /device:TPU:1 before, /device:TPU:8 now
where the time goes in v5:
time: 47.8 us; the launch traced here: 47.7 us
  Pallas kernels  46.4 us (97%)
  between operations  0.64 us (1%)
  local copies, waits for them, and re-layouts  0.63 us (1%)
    pallas_call x1, Pallas kernels, local(): pl.pallas_call(kernel, out_shape=jax.ShapeDtypeStruct((2, 32, 2, 128), F3...  46.4 us

profile of v5, /device:TPU:8, one launch (start us, length us, event | category | flops | bytes accessed | tf_op | source)
XLA Modules:
  0.0 47.7 jit_solution(3130853721189655912)
XLA Ops:
  0.6 46.4 %shard_map.41 = f32[2,32,2,128]{3,2,1,0:T(2,128)S(1)} custom-call(bf16[148,256]{1,0:T(8,128)(2,1)} %tok_ref.1, bf16[592,4096]{1,0:T(8,128)(2,1)} %grad_ref.1), custom_call_target="tpu_custom_call" | custom-call | flops 1241513984 | bytes 4849664 | tf_op jit(solution)/shard_map/pallas_call | solution.py:365
  47.0 0.6 %slice_bitcast_fusion = (f32[2,4096]{1,0:T(2,128)}, f32[2,4096]{1,0:T(2,128)}) fusion(f32[2,2,32,128]{3,1,2,0:T(2,128)S(1)} %bitcast.5), kind=kLoop, calls=%fused_computation | loop fusion | bytes 131072 | tf_op jit(solution)/shard_map/squeeze | solution.py:405

commit v6 on v5

--- a/solution.py
+++ b/solution.py
@@ -21,11 +21,10 @@
 BF16 = jnp.bfloat16
 MESH = pl.DeviceIdType.MESH
 FAR_FIRST = (4, 3, 5, 2, 6, 1, 7)
-RAW_TARGETS = (-4, -3, 3, -1, 1)
-RAW_HOPS = (-2, -1, 1, -1, 1)
-SUM_HOPS = (-2, 2)
-RAW_PARTS = ((0, 1), (2,))
-OWN_PARTS = (3, 4)
+RAW_TARGETS = (-4, -3, 3)
+RAW_HOPS = (-2, -1, 1)
+SUM_HOPS = (-2, 2, -1, 1)
+RAW_PARTS = ((0, 1), (2,), (), ())
 
 
 def row_order(group):
@@ -50,7 +49,7 @@
 def kernel(
     tok_ref, grad_ref, out_ref,
     tok, shifted, order, table, slots, gbuf, turned, part, rot, other, squares,
-    qall, qfirst, q1, q2, inv, land0, code, land1, acc, w, pack, land2,
+    qall, qfirst, q1, q2, inv, ahead, land0, code, land1, acc, w, pack, land2,
     far, gsem, toksem, tsend, trecv, q1send, q1recv, q2send, q2recv, xsend, xrecv, send0, recv0,
     send1, recv1, send2, recv2,
 ):
@@ -181,6 +180,14 @@
             send_sem=q1send, recv_sem=q1recv, device_id=peer, device_id_type=MESH,
         ).start()
 
+    def turn(value):
+        high = value.astype(BF16)
+        low = (value - high.astype(F32)).astype(BF16)
+        return (
+            jnp.dot(high, table[...], preferred_element_type=F32)
+            + jnp.dot(low, table[...], preferred_element_type=F32)
+        ).astype(BF16)
+
     def rotate(half, n):
         g, j = lax.div(n, 2), lax.rem(n, 2)
         rows = pl.ds(pl.multiple_of(half * HALF, HALF), HALF)
@@ -191,12 +198,7 @@
             ],
             axis=0,
         )
-        high = value.astype(BF16)
-        low = (value - high.astype(F32)).astype(BF16)
-        result = (
-            jnp.dot(high, table[...], preferred_element_type=F32)
-            + jnp.dot(low, table[...], preferred_element_type=F32)
-        ).astype(BF16)
+        result = turn(value)
         for m in range(4):
             at = pl.ds(pl.multiple_of(j * 1024 + m * 256, 256), 256)
             rot[g, rows, at] = result[m * HALF:(m + 1) * HALF]
@@ -212,32 +214,44 @@
 
     def raw(g, other_core, j):
         core = shift(c, other_core, 2)
-        place = along(g, RAW_TARGETS[j], core)[0]
-        rows = pl.ds(pl.multiple_of(core * HALF + place * 16, 16), 16)
-        n = other_core * 5 + j
-        return pltpu.make_async_remote_copy(
-            src_ref=rot.at[g, rows, :], dst_ref=land0.at[g, n],
+        n = other_core * 3 + j
+        return pltpu.make_async_remote_copy(
+            src_ref=ahead.at[g, n], dst_ref=land0.at[g, n],
             send_sem=send0.at[g, n], recv_sem=recv0.at[g, n],
             device_id=along(g, RAW_HOPS[j], core)[1], device_id_type=MESH,
         )
+
+    def send_raw(js):
+        chunks = [(j, g, n) for j in js for n in range(2) for g in range(2)]
+        values = []
+        for j, g, n in chunks:
+            core = shift(c, n, 2)
+            place = along(g, RAW_TARGETS[j], core)[0]
+            rows = pl.ds(pl.multiple_of(core * HALF + place * 16, 16), 16)
+            values += [
+                part[rows, g * GROUP + m * 256:g * GROUP + (m + 1) * 256] for m in range(8)
+            ]
+        result = turn(jnp.concatenate(values, axis=0))
+        for i, (j, g, n) in enumerate(chunks):
+            for m in range(8):
+                at = i * 128 + m * 16
+                ahead[g, n * 3 + j, :, m * 256:(m + 1) * 256] = result[at:at + 16]
+            raw(g, n, j).start()
 
     def rotate_theirs(g, carry):
         for j in range(2):
             rotate(oc, 2 * g + j)
             cross(2 * g + j).start()
-        for j in range(5):
-            raw(g, 1, j).start()
         return carry
 
     def rotate_mine(g, carry):
         for j in range(2):
             rotate(c, 2 * g + j)
-        for j in range(5):
-            raw(g, 0, j).start()
         return carry
 
+    send_raw((0,))
+    send_raw((1, 2))
     lax.fori_loop(0, 2, rotate_theirs, 0)
-    lax.fori_loop(0, 2, rotate_mine, 0)
 
     q1_all = pltpu.make_async_remote_copy(
         src_ref=q1.at[pl.ds(1, 15)], dst_ref=q1.at[pl.ds(1, 15)],
@@ -253,6 +267,7 @@
             src_ref=qfirst, dst_ref=q2.at[k],
             send_sem=q2send, recv_sem=q2recv, device_id=peers_y[k - 1], device_id_type=MESH,
         ).start()
+    lax.fori_loop(0, 2, rotate_mine, 0)
     q2_all = pltpu.make_async_remote_copy(
         src_ref=q2.at[pl.ds(1, 7)], dst_ref=q2.at[pl.ds(1, 7)],
         send_sem=q2send, recv_sem=q2recv, device_id=peers_y[0], device_id_type=MESH,
@@ -275,7 +290,7 @@
         value = jnp.clip(rot[g, mine, :].astype(F32) * scale, -1.0, 1.0)
         value = value + jnp.clip(other[g, rows, :].astype(F32) * scale, -1.0, 1.0)
         for j in parts:
-            for n in (j, 5 + j):
+            for n in (j, 3 + j):
                 value = value + jnp.clip(land0[g, n].astype(F32) * scale, -1.0, 1.0)
         return value
 
@@ -291,7 +306,7 @@
             for other_core in range(2):
                 raw(g, other_core, j).wait_recv()
 
-    for n in range(2):
+    for n in range(4):
         def send_sum(g, carry, n=n):
             arrived(g, RAW_PARTS[n])
             code[g, n] = coded(g, SUM_HOPS[n], RAW_PARTS[n]).astype(BF16)
@@ -301,8 +316,7 @@
         lax.fori_loop(0, 2, send_sum, 0)
 
     def keep(g, carry):
-        arrived(g, OWN_PARTS)
-        acc[g] = coded(g, 0, OWN_PARTS)
+        acc[g] = coded(g, 0, ())
         return carry
 
     lax.fori_loop(0, 2, keep, 0)
@@ -317,7 +331,7 @@
 
     for g in range(2):
         value = acc[g]
-        for n in (1, 0):
+        for n in (2, 3, 1, 0):
             first(g, n).wait_recv()
             value = value + land1[g, n].astype(F32)
         acc[g] = value
@@ -351,10 +365,10 @@
     for g in range(2):
         for n in range(2):
             cross(2 * g + n).wait_send()
-        for j in range(5):
+        for j in range(3):
             raw(g, 0, j).wait_send()
             raw(g, 1, j).wait_send()
-        for n in range(2):
+        for n in range(4):
             first(g, n).wait_send()
         for k in FAR_FIRST:
             second(g, k).wait_send()
@@ -384,15 +398,16 @@
             pltpu.VMEM((16, 2, 128), F32),
             pltpu.VMEM((8, 2, 128), F32),
             pltpu.VMEM((2, HALF, 128), F32),
-            pltpu.VMEM((2, 10, 16, GROUP), BF16),
-            pltpu.VMEM((2, 2, 16, GROUP), BF16),
-            pltpu.VMEM((2, 2, 16, GROUP), BF16),
+            pltpu.VMEM((2, 6, 16, GROUP), BF16),
+            pltpu.VMEM((2, 6, 16, GROUP), BF16),
+            pltpu.VMEM((2, 4, 16, GROUP), BF16),
+            pltpu.VMEM((2, 4, 16, GROUP), BF16),
             pltpu.VMEM((2, 16, GROUP), F32),
             pltpu.VMEM((2, 256, 128), F32),
             pltpu.VMEM((2, 8, 32, 128), BF16),
             pltpu.VMEM((2, 8, 32, 128), BF16),
             pltpu.SemaphoreType.REGULAR, dma, dma, dma((NT,)), dma((NT,)), dma, dma, dma, dma, dma((4,)), dma((4,)),
-            dma((2, 10)), dma((2, 10)), dma((2, 2)), dma((2, 2)), dma((2, 8)), dma((2, 8)),
+            dma((2, 6)), dma((2, 6)), dma((2, 4)), dma((2, 4)), dma((2, 8)), dma((2, 8)),
         ],
         compiler_params=pltpu.CompilerParams(
             collective_id=0, has_side_effects=True, vmem_limit_bytes=int(53.85 * 1024 * 1024)

time: 47.8 us -> 44.9 us (0.939)
  the two profiles are of different devices: /device:TPU:8 before, /device:TPU:1 now
where the time goes in v6:
time: 44.9 us; the launch traced here: 44.1 us
  Pallas kernels  42.8 us (95%)
  between operations  0.64 us (1%)
  local copies, waits for them, and re-layouts  0.63 us (1%)
    pallas_call x1, Pallas kernels, local(): pl.pallas_call(kernel, out_shape=jax.ShapeDtypeStruct((2, 32, 2, 128), F3...  42.8 us

profile of v6, /device:TPU:1, one launch (start us, length us, event | category | flops | bytes accessed | tf_op | source)
XLA Modules:
  0.0 44.1 jit_solution(6759816582242459642)
XLA Ops:
  0.6 42.8 %shard_map.41 = f32[2,32,2,128]{3,2,1,0:T(2,128)S(1)} custom-call(bf16[148,256]{1,0:T(8,128)(2,1)} %tok_ref.1, bf16[592,4096]{1,0:T(8,128)(2,1)} %grad_ref.1), custom_call_target="tpu_custom_call" | custom-call | flops 1241513984 | bytes 4849664 | tf_op jit(solution)/shard_map/pallas_call | solution.py:379
  43.4 0.6 %slice_bitcast_fusion = (f32[2,4096]{1,0:T(2,128)}, f32[2,4096]{1,0:T(2,128)}) fusion(f32[2,2,32,128]{3,1,2,0:T(2,128)S(1)} %bitcast.5), kind=kLoop, calls=%fused_computation | loop fusion | bytes 131072 | tf_op jit(solution)/shard_map/squeeze | solution.py:420

commit v7 on v6

--- a/solution.py
+++ b/solution.py
@@ -143,10 +143,11 @@
         ]
 
         def columns(m, carry):
-            g = lax.div(m, 2)
+            g = m // 2 if step == 2 else lax.div(m, 2)
             total = None
             for tile in range(4):
-                at = pl.ds(pl.multiple_of(m * 1024 + tile * 256, 256), 256)
+                at = m * 1024 + tile * 256
+                at = pl.ds(at if step == 2 else pl.multiple_of(at, 256), 256)
                 value = part[:, at] if step > 0 else None
                 for n, depth in enumerate(depths):
                     product = jnp.dot(
@@ -162,23 +163,11 @@
                 squares[m] = total
             return carry
 
-        lax.fori_loop(0, 4, columns, 0)
-    ones = jnp.ones((8, 128), F32)
-    for g in range(2):
-        q = lax.dot_general(
-            ones, squares[2 * g] + squares[2 * g + 1], (((1,), (1,)), ((), ())),
-            preferred_element_type=F32, precision=lax.Precision.HIGHEST,
-        )
-        for half in range(2):
-            qall[half, g:g + 1, :] = q[0:1, half * HALF:(half + 1) * HALF]
-
-    pl.semaphore_wait(far, 4)
-
-    for slot, core, peer in peers_1:
-        pltpu.make_async_remote_copy(
-            src_ref=qall.at[core], dst_ref=q1.at[slot],
-            send_sem=q1send, recv_sem=q1recv, device_id=peer, device_id_type=MESH,
-        ).start()
+        if step == 2:
+            for m in range(4):
+                columns(m, 0)
+        else:
+            lax.fori_loop(0, 4, columns, 0)
 
     def turn(value):
         high = value.astype(BF16)
@@ -250,6 +239,24 @@
         return carry
 
     send_raw((0,))
+
+    ones = jnp.ones((8, 128), F32)
+    for g in range(2):
+        q = lax.dot_general(
+            ones, squares[2 * g] + squares[2 * g + 1], (((1,), (1,)), ((), ())),
+            preferred_element_type=F32, precision=lax.Precision.HIGHEST,
+        )
+        for half in range(2):
+            qall[half, g:g + 1, :] = q[0:1, half * HALF:(half + 1) * HALF]
+
+    pl.semaphore_wait(far, 4)
+
+    for slot, core, peer in peers_1:
+        pltpu.make_async_remote_copy(
+            src_ref=qall.at[core], dst_ref=q1.at[slot],
+            send_sem=q1send, recv_sem=q1recv, device_id=peer, device_id_type=MESH,
+        ).start()
+
     send_raw((1, 2))
     lax.fori_loop(0, 2, rotate_theirs, 0)
 
@@ -344,6 +351,20 @@
         for k in FAR_FIRST:
             second(g, k).start()
 
+    for k in (1, 3):
+        tokens(k).wait_send()
+        pass_on(k).wait_send()
+    q1_all.wait_send()
+    q2_all.wait_send()
+    for g in range(2):
+        for n in range(2):
+            cross(2 * g + n).wait_send()
+        for j in range(3):
+            raw(g, 0, j).wait_send()
+            raw(g, 1, j).wait_send()
+        for n in range(4):
+            first(g, n).wait_send()
+
     for g in range(2):
         total = pack[g, (z, y)[g]].astype(F32)
         for k in FAR_FIRST:
@@ -357,19 +378,7 @@
             out_ref[1, at:at + 16, i, :] = value
             out_ref[0, at:at + 16, i, :] = value * scale
 
-    for k in (1, 3):
-        tokens(k).wait_send()
-        pass_on(k).wait_send()
-    q1_all.wait_send()
-    q2_all.wait_send()
-    for g in range(2):
-        for n in range(2):
-            cross(2 * g + n).wait_send()
-        for j in range(3):
-            raw(g, 0, j).wait_send()
-            raw(g, 1, j).wait_send()
-        for n in range(4):
-            first(g, n).wait_send()
+    for g in range(2):
         for k in FAR_FIRST:
             second(g, k).wait_send()
 

time: 44.9 us -> 45.9 us (1.022)
  Pallas kernels: 42.8 us -> 44.1 us
    pallas_call x1, Pallas kernels: 42.8 us -> 44.1 us  [local(): pl.pallas_call(kernel, out_shape=jax.ShapeDtypeStruct((2, 32, 2, 128), F3...]
where the time goes in v7:
time: 45.9 us; the launch traced here: 45.4 us
  Pallas kernels  44.1 us (96%)
  between operations  0.64 us (1%)
  local copies, waits for them, and re-layouts  0.63 us (1%)
    pallas_call x1, Pallas kernels, local(): pl.pallas_call(kernel, out_shape=jax.ShapeDtypeStruct((2, 32, 2, 128), F3...  44.1 us

profile of v7, /device:TPU:1, one launch (start us, length us, event | category | flops | bytes accessed | tf_op | source)
XLA Modules:
  0.0 45.4 jit_solution(17714886753989402353)
XLA Ops:
  0.6 44.1 %shard_map.41 = f32[2,32,2,128]{3,2,1,0:T(2,128)S(1)} custom-call(bf16[148,256]{1,0:T(8,128)(2,1)} %tok_ref.1, bf16[592,4096]{1,0:T(8,128)(2,1)} %grad_ref.1), custom_call_target="tpu_custom_call" | custom-call | flops 1241513984 | bytes 4849664 | tf_op jit(solution)/shard_map/pallas_call | solution.py:388
  44.8 0.6 %slice_bitcast_fusion = (f32[2,4096]{1,0:T(2,128)}, f32[2,4096]{1,0:T(2,128)}) fusion(f32[2,2,32,128]{3,1,2,0:T(2,128)S(1)} %bitcast.5), kind=kLoop, calls=%fused_computation | loop fusion | bytes 131072 | tf_op jit(solution)/shard_map/squeeze | solution.py:429

commit v8 on v7

--- a/solution.py
+++ b/solution.py
@@ -238,8 +238,6 @@
             rotate(c, 2 * g + j)
         return carry
 
-    send_raw((0,))
-
     ones = jnp.ones((8, 128), F32)
     for g in range(2):
         q = lax.dot_general(
@@ -257,6 +255,7 @@
             send_sem=q1send, recv_sem=q1recv, device_id=peer, device_id_type=MESH,
         ).start()
 
+    send_raw((0,))
     send_raw((1, 2))
     lax.fori_loop(0, 2, rotate_theirs, 0)
 

time: 45.9 us -> 44 us (0.959)
  Pallas kernels: 44.1 us -> 41.9 us
    pallas_call x1, Pallas kernels: 44.1 us -> 41.9 us  [local(): pl.pallas_call(kernel, out_shape=jax.ShapeDtypeStruct((2, 32, 2, 128), F3...]
where the time goes in v8:
time: 44 us; the launch traced here: 43.2 us
  Pallas kernels  41.9 us (95%)
  between operations  0.64 us (1%)
  local copies, waits for them, and re-layouts  0.63 us (1%)
    pallas_call x1, Pallas kernels, local(): pl.pallas_call(kernel, out_shape=jax.ShapeDtypeStruct((2, 32, 2, 128), F3...  41.9 us

profile of v8, /device:TPU:1, one launch (start us, length us, event | category | flops | bytes accessed | tf_op | source)
XLA Modules:
  0.0 43.2 jit_solution(4160338090510490999)
XLA Ops:
  0.6 41.9 %shard_map.41 = f32[2,32,2,128]{3,2,1,0:T(2,128)S(1)} custom-call(bf16[148,256]{1,0:T(8,128)(2,1)} %tok_ref.1, bf16[592,4096]{1,0:T(8,128)(2,1)} %grad_ref.1), custom_call_target="tpu_custom_call" | custom-call | flops 1241513984 | bytes 4849664 | tf_op jit(solution)/shard_map/pallas_call | solution.py:387
  42.6 0.6 %slice_bitcast_fusion = (f32[2,4096]{1,0:T(2,128)}, f32[2,4096]{1,0:T(2,128)}) fusion(f32[2,2,32,128]{3,1,2,0:T(2,128)S(1)} %bitcast.5), kind=kLoop, calls=%fused_computation | loop fusion | bytes 131072 | tf_op jit(solution)/shard_map/squeeze | solution.py:428
